TPU v7x, 32 devices: a whole 2x2x4 slice. The times are simulated.
32 devices in a mesh: dp: 4 (over y, x), ctx: 8 (over z, core).
Axes of the slice: x: 2, y: 2, z: 4, core: 2. Of those that a mesh axis runs over, the one named last changes fastest.
Arguments:
- queries: bfloat16 [4, 2048, 512], P('dp', 'ctx'), may hold values from -6 to 6
- key_vectors: bfloat16 [4, 2048, 512], P('dp', 'ctx'), may hold values from -6 to 6
- value_vectors: bfloat16 [4, 2048, 512], P('dp', 'ctx'), may hold values from -6 to 6
- grad_output: bfloat16 [4, 2048, 512], P('dp', 'ctx'), may hold values from -768 to 768
- pattern: int32 [4, 16, 2], P('dp', 'ctx'), may hold values from 0 to 1
- lengths: int32 [4, 1], P('dp'), may hold values from 512 to 2048, as said below
- widths: int32 [4, 1], P('dp'), may hold values from 1 to 2, as said below
- relative_bucket_bias: float32 [4, 7], replicated, may hold values from -4 to 4
Outputs:
- grad_queries: bfloat16 [4, 2048, 512], P('dp', 'ctx')
- grad_keys: bfloat16 [4, 2048, 512], P('dp', 'ctx')
- value_row_gradients: bfloat16 [4, 2048, 512], P('dp', 'ctx')
- grad_bias: float32 [4, 7], replicated
Inputs may be any that keep to these rules, and one draw needn't show every extreme that they name: `lengths`: one user has a history of all 2048 events and one has 512. `widths`: some user has the widest band and some the narrowest.
All inputs are finite; a program needn't handle non-finite values.
Results may differ from a plain program's by a relative error of at most 0.005.
Values may be sent and summed in bfloat16 or wider, within the bound.
A program may use at most 64 MiB of HBM per device.

v0:
```python
import jax
import jax.numpy as jnp
from jax import lax
from jax.sharding import PartitionSpec as P

BLOCK = 128
GROUP = 8
FAR = 2
NBUCK = 7
SEQ = 2048


def from_behind(array, axis, by):
    size = lax.axis_size(axis)
    pairs = [(i, i + by) for i in range(size) if 0 <= i + by < size]
    return lax.ppermute(array, axis, pairs)


def tile_grads(q_rows, g_rows, k_rows, v_rows, keep_mask, buckets, relative_bucket_bias):
    groups, query_len, model_width = q_rows.shape
    key_len = k_rows.shape[1]
    head_count = relative_bucket_bias.shape[0]
    head_dim = model_width // head_count
    q_blocks = query_len // BLOCK
    k_blocks = key_len // BLOCK
    scaling = head_dim ** (-0.5)
    q_heads = q_rows.reshape(groups, query_len, head_count, head_dim)
    g_heads = g_rows.reshape(groups, query_len, head_count, head_dim)
    k_heads = k_rows.reshape(groups, key_len, head_count, head_dim)
    v_heads = v_rows.reshape(groups, key_len, head_count, head_dim)
    onehot = (buckets[..., None] == jnp.arange(NBUCK, dtype=jnp.int32)).astype(jnp.float32)
    bias_tile = jnp.einsum(
        "gxyu,hu->ghxy", onehot, relative_bucket_bias, precision=lax.Precision.HIGHEST
    )
    raw_score = jnp.einsum("gqhd,gkhd->ghqk", q_heads, k_heads, preferred_element_type=jnp.float32)
    score = (raw_score * scaling).reshape(groups, head_count, q_blocks, BLOCK, k_blocks, BLOCK)
    score = (score + bias_tile[:, :, :, None, :, None]).reshape(
        groups, head_count, query_len, key_len
    )
    keep = keep_mask[:, None, :, :]
    sigmoid_s = jax.nn.sigmoid(score)
    weights_bf = jnp.where(keep, score * sigmoid_s / SEQ, 0.0).astype(jnp.bfloat16)
    value_gradient = jnp.einsum(
        "ghqk,gqhd->gkhd", weights_bf, g_heads, preferred_element_type=jnp.float32
    )
    grad_prob = jnp.einsum("gqhd,gkhd->ghqk", g_heads, v_heads, preferred_element_type=jnp.float32)
    dscore = jnp.where(keep, grad_prob * (sigmoid_s * (1.0 + score * (1.0 - sigmoid_s))) / SEQ, 0.0)
    dscore_bf = dscore.astype(jnp.bfloat16)
    block_sums = dscore.reshape(groups, head_count, q_blocks, BLOCK, k_blocks, BLOCK).sum(
        axis=(3, 5)
    )
    grad_bias = jnp.einsum("ghxy,gxyu->hu", block_sums, onehot, precision=lax.Precision.HIGHEST)
    grad_q = (
        jnp.einsum("ghqk,gkhd->gqhd", dscore_bf, k_heads, preferred_element_type=jnp.float32)
        * scaling
    )
    key_gradient = (
        jnp.einsum("ghqk,gqhd->gkhd", dscore_bf, q_heads, preferred_element_type=jnp.float32)
        * scaling
    )
    return (
        grad_q.reshape(groups, query_len, model_width),
        key_gradient.reshape(groups, key_len, model_width),
        value_gradient.reshape(groups, key_len, model_width),
        grad_bias,
    )


def local_mask(span_id, length, band_width, token_count):
    blocks = token_count // BLOCK
    places = span_id * token_count + jnp.arange(token_count, dtype=jnp.int32)
    block_ids = jnp.arange(token_count, dtype=jnp.int32) // BLOCK
    allowed = (block_ids[:, None] - block_ids[None, :] <= band_width) & (
        places[None, :] <= places[:, None]
    )
    allowed = allowed & (places[:, None] < length) & (places[None, :] < length)
    grid = jnp.arange(blocks, dtype=jnp.int32)
    buckets = jnp.clip(grid[:, None] - grid[None, :], 0, NBUCK - 1)
    return (allowed[None], buckets[None])


def near_mask(span_id, length, band_width, token_count):
    blocks = token_count // BLOCK
    q_places = span_id * token_count + jnp.arange(token_count, dtype=jnp.int32)
    k_places = (span_id - 1) * token_count + jnp.arange(token_count, dtype=jnp.int32)
    block_ids = jnp.arange(token_count, dtype=jnp.int32) // BLOCK
    distance = block_ids[:, None] + blocks - block_ids[None, :]
    allowed = (distance <= band_width) & (q_places[:, None] < length) & (k_places[None, :] < length)
    allowed = allowed & (span_id >= 1) & (span_id < GROUP)
    grid = jnp.arange(blocks, dtype=jnp.int32)
    buckets = jnp.clip(grid[:, None] + blocks - grid[None, :], 0, NBUCK - 1)
    return (allowed[None], buckets[None])


def far_mask(span_id, chosen, distance, length, token_count):
    blocks = token_count // BLOCK
    grid = jnp.arange(blocks, dtype=jnp.int32)
    inner = jnp.arange(BLOCK, dtype=jnp.int32)
    q_places = span_id * token_count + grid[:, None] * BLOCK + inner[None, :]
    k_places = (span_id - distance) * token_count + chosen[:, None] * BLOCK + inner[None, :]
    allowed = (q_places[:, :, None] < length) & (k_places[:, None, :] < length)
    allowed = allowed & (span_id >= distance) & (span_id < GROUP)
    buckets = jnp.clip(distance * blocks + grid - chosen, 0, NBUCK - 1)[:, None, None]
    return (allowed, buckets)


def local_terms(q_rows, g_rows, k_rows, v_rows, span_id, length, band_width, relative_bucket_bias):
    keep_mask, buckets = local_mask(span_id, length, band_width, q_rows.shape[0])
    grads = tile_grads(
        q_rows[None],
        g_rows[None],
        k_rows[None],
        v_rows[None],
        keep_mask,
        buckets,
        relative_bucket_bias,
    )
    return (grads[0][0], grads[1][0], grads[2][0], grads[3])


def near_terms(q_rows, g_rows, k_rows, v_rows, span_id, length, band_width, relative_bucket_bias):
    keep_mask, buckets = near_mask(span_id, length, band_width, q_rows.shape[0])
    grads = tile_grads(
        q_rows[None],
        g_rows[None],
        k_rows[None],
        v_rows[None],
        keep_mask,
        buckets,
        relative_bucket_bias,
    )
    return (grads[0][0], grads[1][0], grads[2][0], grads[3])


def far_terms(
    q_rows, g_rows, k_rows, v_rows, chosen, span_id, distance, length, relative_bucket_bias
):
    token_count, model_width = q_rows.shape
    blocks = token_count // BLOCK
    keep_mask, buckets = far_mask(span_id, chosen, distance, length, token_count)
    q_tiles = q_rows.reshape(blocks, BLOCK, model_width)
    g_tiles = g_rows.reshape(blocks, BLOCK, model_width)
    k_tiles = jnp.take(k_rows.reshape(blocks, BLOCK, model_width), chosen, axis=0)
    v_tiles = jnp.take(v_rows.reshape(blocks, BLOCK, model_width), chosen, axis=0)
    grad_q, key_gradient, value_gradient, grad_bias = tile_grads(
        q_tiles, g_tiles, k_tiles, v_tiles, keep_mask, buckets, relative_bucket_bias
    )
    selector_matrix = (chosen[:, None] == jnp.arange(blocks, dtype=jnp.int32)[None, :]).astype(
        jnp.float32
    )
    key_gradient = jnp.einsum(
        "as,apc->spc", selector_matrix, key_gradient, precision=lax.Precision.HIGHEST
    ).reshape(token_count, model_width)
    value_gradient = jnp.einsum(
        "as,apc->spc", selector_matrix, value_gradient, precision=lax.Precision.HIGHEST
    ).reshape(token_count, model_width)
    return (grad_q.reshape(token_count, model_width), key_gradient, value_gradient, grad_bias)


def on_device(
    queries, key_vectors, value_vectors, grad_output, pattern, lengths, widths, relative_bucket_bias
):
    position = lax.axis_index("ctx")
    span_id = position % GROUP
    user_slot = position // GROUP
    length = lengths[0, user_slot]
    band_width = widths[0, user_slot]
    q_rows = queries[0]
    k_rows = key_vectors[0]
    v_rows = value_vectors[0]
    g_rows = grad_output[0]
    block_table = pattern[0]
    grad_q, key_gradient, value_gradient, grad_bias = local_terms(
        q_rows, g_rows, k_rows, v_rows, span_id, length, band_width, relative_bucket_bias
    )
    distances = [2**section for section in range(FAR + 1)]
    table_bf = block_table.astype(jnp.bfloat16)
    for section, distance in enumerate(distances):
        far_q, far_g, far_table = from_behind((q_rows, g_rows, table_bf), "ctx", -distance)
        query_span = span_id + distance
        if section == 0:
            terms = near_terms(
                far_q, far_g, k_rows, v_rows, query_span, length, band_width, relative_bucket_bias
            )
        else:
            chosen = far_table[:, section - 1].astype(jnp.int32)
            terms = far_terms(
                far_q,
                far_g,
                k_rows,
                v_rows,
                chosen,
                query_span,
                distance,
                length,
                relative_bucket_bias,
            )
        key_gradient = key_gradient + terms[1]
        value_gradient = value_gradient + terms[2]
        grad_bias = grad_bias + terms[3]
        back_q = from_behind(terms[0], "ctx", distance)
        grad_q = grad_q + back_q
    grad_bias = lax.psum(grad_bias, ("dp", "ctx"))
    return (
        grad_q[None].astype(jnp.bfloat16),
        key_gradient[None].astype(jnp.bfloat16),
        value_gradient[None].astype(jnp.bfloat16),
        grad_bias,
    )


def solution(mesh):
    in_specs = (
        P("dp", "ctx", None),
        P("dp", "ctx", None),
        P("dp", "ctx", None),
        P("dp", "ctx", None),
        P("dp", "ctx", None),
        P("dp", None),
        P("dp", None),
        P(),
    )
    out_specs = (P("dp", "ctx", None), P("dp", "ctx", None), P("dp", "ctx", None), P())
    return jax.shard_map(
        on_device, mesh=mesh, in_specs=in_specs, out_specs=out_specs, check_vma=False
    )
```

profile of v0, /device:TPU:12, one launch (start us, length us, event | category | flops | bytes accessed | tf_op | source)
XLA Modules:
  0.0 182.2 jit_solution(13746353603222092864)
XLA Ops:
  1.3 1.4 collective-permute-start.7
  2.8 2.4 %collective-permute-start.3 = (bf16[2,2]{1,0:T(2,128)(2,1)S(1)}, bf16[2,2]{1,0:T(2,128)(2,1)S(1)}, u32[]{:S(2)}, u32[]{:S(2)}) collective-permute-start(bf16[2,2]{1,0:T(2,128)(2,1)S(1)} %convert_bitcast_fusion), channel_id=1, source_target_pairs={{2,0},{3,1},{4,2},{5,3},{6,4},{7,5},{10,8},{11,9},{12,10},{13,11},... | collective-permute-start | bytes 32 | tf_op jit(solution)/shard_map/ppermute | solution.py:16
  5.1 1.8 copy.254
  6.9 1.3 collective-permute-start.8
  8.2 1.9 %collective-permute-start.4 = (bf16[256,512]{0,1:T(8,128)(2,1)}, bf16[256,512]{0,1:T(8,128)(2,1)}, u32[]{:S(2)}, u32[]{:S(2)}) collective-permute-start(bf16[256,512]{0,1:T(8,128)(2,1)} %bitcast.8), channel_id=1, source_target_pairs={{2,0},{3,1},{4,2},{5,3},{6,4},{7,5},{10,8},{11,9},{12,10},{13,11},... | collective-permute-start | bytes 786440 | tf_op jit(solution)/shard_map/ppermute | solution.py:16
  10.1 1.9 %collective-permute-start = (bf16[256,512]{0,1:T(8,128)(2,1)}, bf16[256,512]{0,1:T(8,128)(2,1)}, u32[]{:S(2)}, u32[]{:S(2)}) collective-permute-start(bf16[256,512]{0,1:T(8,128)(2,1)} %bitcast.8), channel_id=1, source_target_pairs={{1,0},{2,1},{3,2},{4,3},{5,4},{6,5},{7,6},{9,8},{10,9},{11,10},{12... | collective-permute-start | bytes 786440 | tf_op jit(solution)/shard_map/ppermute | solution.py:16
  13.9 0.9 copy.171
  16.9 0.8 add.425
  18.4 2.3 %fusion.27 = f32[4,256,128]{1,2,0:T(8,128)} fusion(bf16[256,4,128]{0,2,1:T(8,128)(2,1)} %bitcast.83, f32[4,256,256]{2,1,0:T(8,128)S(1)} %fusion.3, pred[256,256]{1,0:T(8,128)(4,1)S(1)} %get-tuple-element.10), kind=kOutput, calls=%fused_computation.68 | convolution fusion | flops 68943872 | bytes 1900544 | tf_op jit(solution)/shard_map/ghqk,gqhd->gkhd/dot_general | solution.py:43
  20.6 1.6 fusion.5
  22.3 1.0 fusion.33
  24.8 1.3 add.435
  26.1 2.1 %add.436 = f32[4,256,256]{2,1,0:T(8,128)S(1)} reshape(f32[4,2,128,2,128]{4,3,2,1,0:T(2,128)} %add.435) | data formatting | bytes 2097152 | tf_op jit(solution)/shard_map/add | solution.py:37
  28.2 2.1 %convolution_multiply_fusion.11 = f32[4,256,128]{1,2,0:T(8,128)} fusion(bf16[256,4,128]{0,2,1:T(8,128)(2,1)} %copy.171, f32[4,256,256]{2,1,0:T(8,128)S(1)} %fusion.5), kind=kOutput, calls=%fused_computation.40 | convolution fusion | flops 67502080 | bytes 1835008 | tf_op jit(solution)/shard_map/ghqk,gkhd->gqhd/dot_general | solution.py:54
  30.3 2.0 %copy.181 = f32[256,512]{1,0:T(8,128)} copy(f32[256,512]{0,1:T(8,128)} %bitcast.209) | data formatting | bytes 1048576 | tf_op jit(solution)/shard_map/squeeze;reshape | solution.py:118
  33.3 1.3 collective-permute-start.9
  34.8 1.9 %collective-permute-start.5 = (bf16[256,512]{0,1:T(8,128)(2,1)S(1)}, bf16[256,512]{0,1:T(8,128)(2,1)}, u32[]{:S(2)}, u32[]{:S(2)}) collective-permute-start(bf16[256,512]{0,1:T(8,128)(2,1)S(1)} %bitcast.194), channel_id=1, source_target_pairs={{2,0},{3,1},{4,2},{5,3},{6,4},{7,5},{10,8},{11,9},{12,10},{13,11},... | collective-permute-start | bytes 786440 | tf_op jit(solution)/shard_map/ppermute | solution.py:16
  41.7 0.8 copy.183
  42.8 0.8 copy.193
  43.8 11.9 %collective-permute-done.5 = bf16[256,512]{0,1:T(8,128)(2,1)} collective-permute-done((bf16[256,512]{0,1:T(8,128)(2,1)S(1)}, bf16[256,512]{0,1:T(8,128)(2,1)}, u32[]{:S(2)}, u32[]{:S(2)}) %collective-permute-start.5) | collective-permute-done | bytes 262176 | tf_op jit(solution)/shard_map/ppermute | solution.py:16
  55.7 2.1 %collective-permute-start.1 = (bf16[256,512]{0,1:T(8,128)(2,1)S(1)}, bf16[256,512]{0,1:T(8,128)(2,1)S(1)}, u32[]{:S(2)}, u32[]{:S(2)}) collective-permute-start(bf16[256,512]{0,1:T(8,128)(2,1)S(1)} %bitcast.195), channel_id=1, source_target_pairs={{1,0},{2,1},{3,2},{4,3},{5,4},{6,5},{7,6},{9,8},{10,9},{11,10},{12... | collective-permute-start | bytes 786440 | tf_op jit(solution)/shard_map/ppermute | solution.py:16
  57.8 1.0 reshape.841
  59.7 1.7 reshape.840
  61.4 2.1 %fusion.107 = (f32[2,4]{1,0:T(2,128)}, bf16[2,4,128,128]{2,3,1,0:T(8,128)(2,1)S(1)}) fusion(f32[2,4,128,128]{2,3,1,0:T(8,128)S(1)} %fusion.19, bf16[2,128,4,128]{1,3,2,0:T(8,128)(2,1)} %bitcast.221, bf16[2,128,4,128]{1,0,3,2:T(2,128)(2,1)} %reshape.840, pred[2,128,128]{1,2,0:T(8,128)(4,1)S(1)} %and_and_fusion.1), kind=kOutput, calls=%fused_computation.191 | convolution fusion | flops 35127288 | bytes 1343520 | tf_op jit(solution)/shard_map/gqhd,gkhd->ghqk/dot_general | solution.py:46
  63.6 1.1 fusion.13
  64.7 1.0 fusion.17
  65.7 1.0 reshape.843
  67.4 1.1 fusion.16
  68.5 1.8 reshape.842
  70.3 2.2 %fusion.108 = (f32[2,4]{1,0:T(2,128)}, bf16[2,4,128,128]{2,3,1,0:T(8,128)(2,1)S(1)}) fusion(f32[2,4,128,128]{2,3,1,0:T(8,128)} %fusion.16, bf16[2,128,4,128]{1,3,2,0:T(8,128)(2,1)S(1)} %bitcast.220, bf16[2,128,4,128]{1,0,3,2:T(2,128)(2,1)} %reshape.842, pred[2,128,128]{1,2,0:T(8,128)(4,1)S(1)} %and_and_fusion), kind=kOutput, calls=%fused_computation.192 | convolution fusion | flops 35127288 | bytes 1343520 | tf_op jit(solution)/shard_map/gqhd,gkhd->ghqk/dot_general | solution.py:46
  72.4 1.1 fusion.12
  73.5 1.1 fusion.36
  75.1 1.0 fusion.14
  76.7 1.1 fusion.37
  77.9 1.6 fusion.2
  80.4 1.3 copy.219
  81.6 1.1 fusion.71
  82.8 2.0 %copy.191 = f32[2,128,4,128]{3,2,1,0:T(4,128)} copy(f32[2,128,4,128]{1,3,2,0:T(8,128)} %fusion.17) | data formatting | bytes 1048576 | tf_op jit(solution)/shard_map/mul | solution.py:54
  84.9 1.9 %copy.293 = f32[32,8,4,128]{3,1,2,0:T(8,128)} copy(f32[32,8,4,128]{3,2,1,0:T(4,128)} %bitcast.210) | data formatting | bytes 1048576
  86.7 2.0 %copy.206 = f32[2,128,4,128]{1,3,2,0:T(8,128)} copy(f32[2,128,4,128]{3,1,2,0:T(8,128)} %fusion.13) | data formatting | bytes 1048576 | tf_op jit(solution)/shard_map/mul | solution.py:58
  88.8 2.0 %copy.207 = f32[2,128,512]{2,0,1:T(2,128)} copy(f32[2,128,512]{1,2,0:T(8,128)} %bitcast.211) | data formatting | bytes 1048576 | tf_op jit(solution)/shard_map/reshape | solution.py:63
  90.8 2.1 %fusion.73 = f32[2,128,512]{2,0,1:T(2,128)S(1)} fusion(f32[2,128,512]{2,0,1:T(2,128)} %copy.207, s32[2]{0:T(128)S(1)} %get-tuple-element.6), kind=kOutput, calls=%fused_computation.131 | convolution fusion | flops 3145732 | bytes 1048584 | tf_op jit(solution)/shard_map/as,apc->spc/dot_general | solution.py:151
  92.9 0.9 copy.208
  93.8 2.0 %copy.224 = f32[2,128,512]{2,0,1:T(2,128)} copy(f32[2,128,512]{1,2,0:T(8,128)} %bitcast.217) | data formatting | bytes 1048576 | tf_op jit(solution)/shard_map/reshape | solution.py:64
  95.9 2.1 %fusion.67 = f32[2,128,512]{2,0,1:T(2,128)S(1)} fusion(f32[2,128,512]{2,0,1:T(2,128)} %copy.224, s32[2]{0:T(128)S(1)} %get-tuple-element.8), kind=kOutput, calls=%fused_computation.125 | convolution fusion | flops 3145732 | bytes 1048584 | tf_op jit(solution)/shard_map/as,apc->spc/dot_general | solution.py:154
  98.0 0.9 copy.225
  98.9 2.0 %copy.201 = f32[2,128,4,128]{3,2,1,0:T(4,128)} copy(f32[2,128,4,128]{1,3,2,0:T(8,128)} %fusion.14) | data formatting | bytes 1048576 | tf_op jit(solution)/shard_map/mul | solution.py:54
  100.9 1.9 %copy.292 = f32[32,8,4,128]{3,1,2,0:T(8,128)} copy(f32[32,8,4,128]{3,2,1,0:T(4,128)} %bitcast.212) | data formatting | bytes 1048576
  102.8 2.0 %copy.213 = f32[2,128,4,128]{1,3,2,0:T(8,128)} copy(f32[2,128,4,128]{3,1,2,0:T(8,128)} %fusion.12) | data formatting | bytes 1048576 | tf_op jit(solution)/shard_map/mul | solution.py:58
  104.8 2.0 %copy.214 = f32[2,128,512]{2,0,1:T(2,128)} copy(f32[2,128,512]{1,2,0:T(8,128)} %bitcast.213) | data formatting | bytes 1048576 | tf_op jit(solution)/shard_map/reshape | solution.py:63
  106.9 2.2 %fusion.69 = f32[2,128,512]{2,0,1:T(2,128)S(1)} fusion(f32[2,128,512]{2,0,1:T(2,128)} %copy.214, s32[2]{0:T(128)S(1)} %get-tuple-element.8), kind=kOutput, calls=%fused_computation.127 | convolution fusion | flops 3145732 | bytes 1048584 | tf_op jit(solution)/shard_map/as,apc->spc/dot_general | solution.py:151
  109.1 0.9 copy.215
  110.0 3.1 %collective-permute-start.10 = (f32[256,512]{1,0:T(8,128)}, f32[256,512]{1,0:T(8,128)}, u32[]{:S(2)}, u32[]{:S(2)}) collective-permute-start(f32[256,512]{1,0:T(8,128)} %bitcast.181), channel_id=1, source_target_pairs={{0,4},{1,5},{2,6},{3,7},{8,12},{9,13},{10,14},{11,15},{16,20},{17,... | collective-permute-start | bytes 1572872 | tf_op jit(solution)/shard_map/ppermute | solution.py:16
  113.1 2.1 %collective-permute-start.6 = (f32[256,512]{1,0:T(8,128)}, f32[256,512]{1,0:T(8,128)}, u32[]{:S(2)}, u32[]{:S(2)}) collective-permute-start(f32[256,512]{1,0:T(8,128)} %bitcast.182), channel_id=1, source_target_pairs={{0,2},{1,3},{2,4},{3,5},{4,6},{5,7},{8,10},{9,11},{10,12},{11,13},... | collective-permute-start | bytes 1572872 | tf_op jit(solution)/shard_map/ppermute | solution.py:16
  115.2 2.2 %convolution_add_fusion = f32[4,256,128]{1,2,0:T(8,128)} fusion(f32[4,256,128]{1,2,0:T(8,128)S(1)} %copy-done.35, bf16[256,4,128]{0,2,1:T(8,128)(2,1)} %bitcast.9, f32[4,256,256]{2,1,0:T(8,128)S(1)} %copy-done.15, pred[256,256]{1,0:T(8,128)(4,1)S(1)} %get-tuple-element.9), kind=kOutput, calls=%fused_computation.36 | convolution fusion | flops 69074944 | bytes 2424832 | tf_op jit(solution)/shard_map/ghqk,gqhd->gkhd/dot_general | solution.py:43
  117.4 2.0 %copy.221 = f32[1,256,512]{2,1,0:T(8,128)} copy(f32[1,256,512]{1,2,0:T(8,128)} %bitcast.219) | data formatting | bytes 1048576 | tf_op jit(solution)/shard_map/add | solution.py:199
  119.5 2.1 %fusion.20 = f32[4,256,128]{1,2,0:T(8,128)} fusion(f32[4,256,128]{1,2,0:T(8,128)} %fusion.33, bf16[256,4,128]{0,2,1:T(8,128)(2,1)S(1)} %bitcast.216, f32[4,256,256]{2,1,0:T(8,128)S(1)} %fusion.2), kind=kOutput, calls=%fused_computation.38 | convolution fusion | flops 67633152 | bytes 2359296 | tf_op jit(solution)/shard_map/ghqk,gqhd->gkhd/dot_general | solution.py:58
  121.6 1.2 copy.209
  126.1 1.0 copy.180
  127.2 42.2 %psum.7 = f32[4,7]{1,0:T(4,128)} all-reduce(f32[4,7]{1,0:T(4,128)S(1)} %convolution_add_fusion.2), channel_id=1, replica_groups=mesh['dp'=4,'ctx'=8] {'dp','ctx'}, use_global_device_ids=true, to_apply=%region_4.6 | all-reduce | flops 28 | bytes 224 | tf_op jit(solution)/shard_map/psum | solution.py:203
  169.4 1.9 %collective-permute-start.2 = (f32[256,512]{1,0:T(8,128)}, f32[256,512]{1,0:T(8,128)S(1)}, u32[]{:S(2)}, u32[]{:S(2)}) collective-permute-start(f32[256,512]{1,0:T(8,128)} %copy.180), channel_id=1, source_target_pairs={{0,1},{1,2},{2,3},{3,4},{4,5},{5,6},{6,7},{8,9},{9,10},{10,11},{11... | collective-permute-start | bytes 1572872 | tf_op jit(solution)/shard_map/ppermute | solution.py:16
  171.4 0.8 fusion.22
  173.5 6.6 %collective-permute-done.2 = f32[256,512]{1,0:T(8,128)S(1)} collective-permute-done((f32[256,512]{1,0:T(8,128)}, f32[256,512]{1,0:T(8,128)S(1)}, u32[]{:S(2)}, u32[]{:S(2)}) %collective-permute-start.2) | collective-permute-done | bytes 524320 | tf_op jit(solution)/shard_map/ppermute | solution.py:16
  180.1 2.1 %fusion.30 = bf16[1,256,512]{2,1,0:T(8,128)(2,1)} fusion(f32[256,512]{1,0:T(8,128)} %collective-permute-done.10, f32[256,512]{1,0:T(8,128)} %collective-permute-done.6, f32[256,512]{1,0:T(8,128)S(1)} %copy-done.13, f32[256,512]{1,0:T(8,128)S(1)} %collective-permute-done.2), kind=kLoop, calls=%fused_computation.71 | loop fusion | flops 524288 | bytes 2359296 | tf_op jit(solution)/shard_map/convert_element_type | solution.py:205
  (135 shorter events, 19.9 us)
Async XLA Ops:
  0.6 12.8 %copy-start = (f32[4,7]{1,0:T(4,128)S(1)}, f32[4,7]{1,0:T(4,128)}, u32[]{:S(2)}) copy-start(f32[4,7]{1,0:T(4,128)} %param.17) | copy-start | bytes 340
  1.3 12.4 %copy-start.7 = (bf16[1,256,512]{2,1,0:T(8,128)(2,1)S(1)}, bf16[1,256,512]{2,1,0:T(8,128)(2,1)}, u32[]{:S(2)}) copy-start(bf16[1,256,512]{2,1,0:T(8,128)(2,1)} %param.11) | copy-start | bytes 786436
  1.3 31.4 %collective-permute-start.7 = (bf16[2,2]{1,0:T(2,128)(2,1)S(1)}, bf16[2,2]{1,0:T(2,128)(2,1)S(1)}, u32[]{:S(2)}, u32[]{:S(2)}) collective-permute-start(bf16[2,2]{1,0:T(2,128)(2,1)S(1)} %convert_bitcast_fusion), channel_id=1, source_target_pairs={{4,0},{5,1},{6,2},{7,3},{12,8},{13,9},{14,10},{15,11},{20,16},{21,... | collective-permute-start | bytes 32 | tf_op jit(solution)/shard_map/ppermute | solution.py:16
  2.8 32.0 %collective-permute-start.3 = (bf16[2,2]{1,0:T(2,128)(2,1)S(1)}, bf16[2,2]{1,0:T(2,128)(2,1)S(1)}, u32[]{:S(2)}, u32[]{:S(2)}) collective-permute-start(bf16[2,2]{1,0:T(2,128)(2,1)S(1)} %convert_bitcast_fusion), channel_id=1, source_target_pairs={{2,0},{3,1},{4,2},{5,3},{6,4},{7,5},{10,8},{11,9},{12,10},{13,11},... | collective-permute-start | bytes 32 | tf_op jit(solution)/shard_map/ppermute | solution.py:16
  6.9 61.6 %collective-permute-start.8 = (bf16[256,512]{0,1:T(8,128)(2,1)}, bf16[256,512]{0,1:T(8,128)(2,1)}, u32[]{:S(2)}, u32[]{:S(2)}) collective-permute-start(bf16[256,512]{0,1:T(8,128)(2,1)} %bitcast.8), channel_id=1, source_target_pairs={{4,0},{5,1},{6,2},{7,3},{12,8},{13,9},{14,10},{15,11},{20,16},{21,... | collective-permute-start | bytes 786440 | tf_op jit(solution)/shard_map/ppermute | solution.py:16
  8.2 51.5 %collective-permute-start.4 = (bf16[256,512]{0,1:T(8,128)(2,1)}, bf16[256,512]{0,1:T(8,128)(2,1)}, u32[]{:S(2)}, u32[]{:S(2)}) collective-permute-start(bf16[256,512]{0,1:T(8,128)(2,1)} %bitcast.8), channel_id=1, source_target_pairs={{2,0},{3,1},{4,2},{5,3},{6,4},{7,5},{10,8},{11,9},{12,10},{13,11},... | collective-permute-start | bytes 786440 | tf_op jit(solution)/shard_map/ppermute | solution.py:16
  10.1 67.7 %collective-permute-start = (bf16[256,512]{0,1:T(8,128)(2,1)}, bf16[256,512]{0,1:T(8,128)(2,1)}, u32[]{:S(2)}, u32[]{:S(2)}) collective-permute-start(bf16[256,512]{0,1:T(8,128)(2,1)} %bitcast.8), channel_id=1, source_target_pairs={{1,0},{2,1},{3,2},{4,3},{5,4},{6,5},{7,6},{9,8},{10,9},{11,10},{12... | collective-permute-start | bytes 786440 | tf_op jit(solution)/shard_map/ppermute | solution.py:16
  12.1 1.3 copy-start.31
  13.8 1.0 copy-start.17
  14.8 0.9 copy-start.5
  15.7 2.0 %copy-start.2 = (bf16[1,256,512]{1,2,0:T(8,128)(2,1)}, bf16[1,256,512]{1,2,0:T(8,128)(2,1)S(1)}, u32[]{:S(2)}) copy-start(bf16[1,256,512]{1,2,0:T(8,128)(2,1)S(1)} %copy.255) | copy-start | bytes 786436
  18.4 2.3 %copy-start.18 = (bf16[256,4,128]{2,1,0:T(4,128)(2,1)S(1)}, bf16[256,4,128]{2,1,0:T(4,128)(2,1)}, u32[]{:S(2)}) copy-start(bf16[256,4,128]{2,1,0:T(4,128)(2,1)} %reshape.770) | copy-start | bytes 786436
  20.6 1.6 copy-start.3
  23.9 0.6 copy-start.25
  32.3 0.9 copy-start.4
  32.3 4.6 %copy-start.6 = (bf16[1,256,512]{2,1,0:T(8,128)(2,1)S(1)}, bf16[1,256,512]{2,1,0:T(8,128)(2,1)}, u32[]{:S(2)}) copy-start(bf16[1,256,512]{2,1,0:T(8,128)(2,1)} %param.12) | copy-start | bytes 786436
  33.3 32.4 %collective-permute-start.9 = (bf16[256,512]{0,1:T(8,128)(2,1)S(1)}, bf16[256,512]{0,1:T(8,128)(2,1)}, u32[]{:S(2)}, u32[]{:S(2)}) collective-permute-start(bf16[256,512]{0,1:T(8,128)(2,1)S(1)} %bitcast.193), channel_id=1, source_target_pairs={{4,0},{5,1},{6,2},{7,3},{12,8},{13,9},{14,10},{15,11},{20,16},{21,... | collective-permute-start | bytes 786440 | tf_op jit(solution)/shard_map/ppermute | solution.py:16
  34.8 5.5 %copy-start.27 = (s32[2]{0:T(128)}, s32[2]{0:T(128)S(1)}, u32[]{:S(2)}) copy-start(s32[2]{0:T(128)S(1)} %get-tuple-element.15) | copy-start | bytes 28
  34.8 20.9 %collective-permute-start.5 = (bf16[256,512]{0,1:T(8,128)(2,1)S(1)}, bf16[256,512]{0,1:T(8,128)(2,1)}, u32[]{:S(2)}, u32[]{:S(2)}) collective-permute-start(bf16[256,512]{0,1:T(8,128)(2,1)S(1)} %bitcast.194), channel_id=1, source_target_pairs={{2,0},{3,1},{4,2},{5,3},{6,4},{7,5},{10,8},{11,9},{12,10},{13,11},... | collective-permute-start | bytes 786440 | tf_op jit(solution)/shard_map/ppermute | solution.py:16
  36.9 4.1 %copy-start.29 = (s32[2]{0:T(128)}, s32[2]{0:T(128)S(1)}, u32[]{:S(2)}) copy-start(s32[2]{0:T(128)S(1)} %get-tuple-element.11) | copy-start | bytes 28
  36.9 1.0 copy-start.8
  55.7 19.0 %collective-permute-start.1 = (bf16[256,512]{0,1:T(8,128)(2,1)S(1)}, bf16[256,512]{0,1:T(8,128)(2,1)S(1)}, u32[]{:S(2)}, u32[]{:S(2)}) collective-permute-start(bf16[256,512]{0,1:T(8,128)(2,1)S(1)} %bitcast.195), channel_id=1, source_target_pairs={{1,0},{2,1},{3,2},{4,3},{5,4},{6,5},{7,6},{9,8},{10,9},{11,10},{12... | collective-permute-start | bytes 786440 | tf_op jit(solution)/shard_map/ppermute | solution.py:16
  58.8 0.7 copy-start.24
  66.7 0.7 copy-start.23
  68.5 1.8 copy-start.20
  72.4 1.1 copy-start.21
  75.0 2.8 %copy-start.14 = (f32[4,256,256]{2,1,0:T(8,128)}, f32[4,256,256]{2,1,0:T(8,128)S(1)}, u32[]{:S(2)}) copy-start(f32[4,256,256]{2,1,0:T(8,128)S(1)} %fusion) | copy-start | bytes 3145732
  75.0 1.4 copy-start.16
  75.0 1.7 copy-start.22
  76.7 1.2 copy-start.19
  77.9 1.6 copy-start.1
  106.9 8.3 %copy-start.15 = (f32[4,256,256]{2,1,0:T(8,128)S(1)}, f32[4,256,256]{2,1,0:T(8,128)}, u32[]{:S(2)}) copy-start(f32[4,256,256]{2,1,0:T(8,128)} %copy-done.14) | copy-start | bytes 3145732
  109.1 6.2 %copy-start.35 = (f32[4,256,128]{1,2,0:T(8,128)S(1)}, f32[4,256,128]{1,2,0:T(8,128)}, u32[]{:S(2)}) copy-start(f32[4,256,128]{1,2,0:T(8,128)} %fusion.27) | copy-start | bytes 1572868
  110.0 63.5 %collective-permute-start.10 = (f32[256,512]{1,0:T(8,128)}, f32[256,512]{1,0:T(8,128)}, u32[]{:S(2)}, u32[]{:S(2)}) collective-permute-start(f32[256,512]{1,0:T(8,128)} %bitcast.181), channel_id=1, source_target_pairs={{0,4},{1,5},{2,6},{3,7},{8,12},{9,13},{10,14},{11,15},{16,20},{17,... | collective-permute-start | bytes 1572872 | tf_op jit(solution)/shard_map/ppermute | solution.py:16
  113.1 60.4 %collective-permute-start.6 = (f32[256,512]{1,0:T(8,128)}, f32[256,512]{1,0:T(8,128)}, u32[]{:S(2)}, u32[]{:S(2)}) collective-permute-start(f32[256,512]{1,0:T(8,128)} %bitcast.182), channel_id=1, source_target_pairs={{0,2},{1,3},{2,4},{3,5},{4,6},{5,7},{8,10},{9,11},{10,12},{11,13},... | collective-permute-start | bytes 1572872 | tf_op jit(solution)/shard_map/ppermute | solution.py:16
  122.8 0.7 copy-start.26
  123.5 0.7 copy-start.32
  124.3 0.6 copy-start.30
  124.3 0.7 copy-start.33
  125.2 0.7 copy-start.28
  125.2 0.7 copy-start.34
  126.1 45.2 %copy-start.10 = (f32[2,128,512]{2,1,0:T(8,128)S(1)}, f32[2,128,512]{2,1,0:T(8,128)}, u32[]{:S(2)}) copy-start(f32[2,128,512]{2,1,0:T(8,128)} %copy.225) | copy-start | bytes 1572868
  126.1 45.2 %copy-start.12 = (f32[1,256,512]{2,1,0:T(8,128)S(1)}, f32[1,256,512]{2,1,0:T(8,128)}, u32[]{:S(2)}) copy-start(f32[1,256,512]{2,1,0:T(8,128)} %copy.221) | copy-start | bytes 1572868
  169.4 10.7 %collective-permute-start.2 = (f32[256,512]{1,0:T(8,128)}, f32[256,512]{1,0:T(8,128)S(1)}, u32[]{:S(2)}, u32[]{:S(2)}) collective-permute-start(f32[256,512]{1,0:T(8,128)} %copy.180), channel_id=1, source_target_pairs={{0,1},{1,2},{2,3},{3,4},{4,5},{5,6},{6,7},{8,9},{9,10},{10,11},{11... | collective-permute-start | bytes 1572872 | tf_op jit(solution)/shard_map/ppermute | solution.py:16
  171.3 1.0 copy-start.9
  171.3 1.3 copy-start.11
  172.6 7.5 %copy-start.13 = (f32[256,512]{1,0:T(8,128)S(1)}, f32[256,512]{1,0:T(8,128)}, u32[]{:S(2)}) copy-start(f32[256,512]{1,0:T(8,128)} %copy.181) | copy-start | bytes 1572868
where the time goes:
time: 184 us; the launch traced here: 182 us
  local copies, waits for them, and re-layouts  54.7 us (30%)
  blocking collectives  42.2 us (23%)
  matrix products  36.1 us (20%)
  starting transfers between devices  21.3 us (12%)
  waiting for transfers between devices  18.6 us (10%)
  other arithmetic  6.7 us (4%)
  between operations  2.64 us (1%)
    psum x1, blocking collectives, on_device(): grad_bias = lax.psum(grad_bias, ('dp', 'ctx'))  42.2 us
    ppermute x11, starting transfers between devices, from_behind(): return lax.ppermute(array, axis, pairs)  21.3 us
    ppermute x11, waiting for transfers between devices, from_behind(): return lax.ppermute(array, axis, pairs)  18.6 us
    unnamed x74, local copies, waits for them, and re-layouts  10.7 us
    dot_general x4, matrix products, tile_grads(): jnp.einsum('gqhd,gkhd->ghqk', g_heads, v_heads, preferred_element_type=jn...  7.51 us
    dot_general x4, matrix products, tile_grads(): jnp.einsum('ghqk,gqhd->gkhd', weights_bf, g_heads, preferred_element_type...  6.73 us
    dot_general x4, matrix products, tile_grads(): jnp.einsum('ghqk,gqhd->gkhd', dscore_bf, q_heads, preferred_element_type=...  5.31 us
    add x4, local copies, waits for them, and re-layouts, tile_grads(): score + bias_tile[:, :, :, None, :, None]  4.55 us
  transfers between devices with their start and end apart: 11, of which 2 were waited for; matrix products, arithmetic and copies ran while one was open for 31% of the time, Pallas kernels for 0%

commit v1 on v0

--- a/solution.py
+++ b/solution.py
@@ -200,7 +200,8 @@
         grad_bias = grad_bias + terms[3]
         back_q = from_behind(terms[0], "ctx", distance)
         grad_q = grad_q + back_q
-    grad_bias = lax.psum(grad_bias, ("dp", "ctx"))
+    half = lax.psum(grad_bias, "ctx")
+    grad_bias = lax.psum(half, "dp")
     return (
         grad_q[None].astype(jnp.bfloat16),
         key_gradient[None].astype(jnp.bfloat16),

time: 184 us -> 173 us (0.940); the launches traced: 182 us -> 169 us
  blocking collectives: 42.2 us -> 33 us
  matrix products: 36.1 us -> 34.2 us
    psum x1 -> x2, blocking collectives: 42.2 us -> 33 us  [the longest x1 23.5 us: on_device(): half = lax.psum(grad_bias, 'ctx')]
    unnamed x74 -> x80, local copies, waits for them, and re-layouts: 10.7 us -> 10.4 us
  transfers between devices with their start and end apart: 11 -> 11, of which waited for: 2 -> 2; matrix products, arithmetic and copies ran while one was open for 31% -> 33% of each run, Pallas kernels for 0% -> 0%
where the time goes in v1:
time: 173 us; the launch traced here: 169 us
  local copies, waits for them, and re-layouts  52.9 us (31%)
  matrix products  34.2 us (20%)
  blocking collectives  33 us (19%)
  starting transfers between devices  21.1 us (12%)
  waiting for transfers between devices  18.5 us (11%)
  other arithmetic  6.7 us (4%)
  between operations  2.66 us (2%)
    psum x1, blocking collectives, on_device(): half = lax.psum(grad_bias, 'ctx')  23.5 us
    ppermute x11, starting transfers between devices, from_behind(): return lax.ppermute(array, axis, pairs)  21.1 us
    ppermute x11, waiting for transfers between devices, from_behind(): return lax.ppermute(array, axis, pairs)  18.5 us
    unnamed x80, local copies, waits for them, and re-layouts  10.4 us
    psum x1, blocking collectives, on_device(): grad_bias = lax.psum(half, 'dp')  9.51 us
    dot_general x4, matrix products, tile_grads(): jnp.einsum('gqhd,gkhd->ghqk', g_heads, v_heads, preferred_element_type=jn...  7.41 us
    dot_general x4, matrix products, tile_grads(): jnp.einsum('ghqk,gqhd->gkhd', weights_bf, g_heads, preferred_element_type...  6.73 us
    dot_general x4, matrix products, tile_grads(): jnp.einsum('ghqk,gkhd->gqhd', dscore_bf, k_heads, preferred_element_type=...  5.19 us
  transfers between devices with their start and end apart: 11, of which 2 were waited for; matrix products, arithmetic and copies ran while one was open for 33% of the time, Pallas kernels for 0%

profile of v1, /device:TPU:12, one launch (start us, length us, event | category | flops | bytes accessed | tf_op | source)
XLA Modules:
  0.0 169.1 jit_solution(1535710874003048845)
XLA Ops:
  1.3 1.4 collective-permute-start.7
  2.8 2.4 %collective-permute-start.3 = (bf16[2,2]{1,0:T(2,128)(2,1)S(1)}, bf16[2,2]{1,0:T(2,128)(2,1)S(1)}, u32[]{:S(2)}, u32[]{:S(2)}) collective-permute-start(bf16[2,2]{1,0:T(2,128)(2,1)S(1)} %convert_bitcast_fusion), channel_id=1, source_target_pairs={{2,0},{3,1},{4,2},{5,3},{6,4},{7,5},{10,8},{11,9},{12,10},{13,11},... | collective-permute-start | bytes 32 | tf_op jit(solution)/shard_map/ppermute | solution.py:16
  5.1 1.8 %copy.254 = bf16[1,256,512]{1,2,0:T(8,128)(2,1)} copy(bf16[1,256,512]{2,1,0:T(8,128)(2,1)} %param.13) | data formatting | bytes 524288 | tf_op jit(solution)/shard_map/reshape.2
  6.9 1.3 collective-permute-start.8
  8.2 1.9 %collective-permute-start.4 = (bf16[256,512]{0,1:T(8,128)(2,1)}, bf16[256,512]{0,1:T(8,128)(2,1)}, u32[]{:S(2)}, u32[]{:S(2)}) collective-permute-start(bf16[256,512]{0,1:T(8,128)(2,1)} %bitcast.8), channel_id=1, source_target_pairs={{2,0},{3,1},{4,2},{5,3},{6,4},{7,5},{10,8},{11,9},{12,10},{13,11},... | collective-permute-start | bytes 786440 | tf_op jit(solution)/shard_map/ppermute | solution.py:16
  10.1 1.9 %collective-permute-start = (bf16[256,512]{0,1:T(8,128)(2,1)}, bf16[256,512]{0,1:T(8,128)(2,1)}, u32[]{:S(2)}, u32[]{:S(2)}) collective-permute-start(bf16[256,512]{0,1:T(8,128)(2,1)} %bitcast.8), channel_id=1, source_target_pairs={{1,0},{2,1},{3,2},{4,3},{5,4},{6,5},{7,6},{9,8},{10,9},{11,10},{12... | collective-permute-start | bytes 786440 | tf_op jit(solution)/shard_map/ppermute | solution.py:16
  13.9 0.9 copy.171
  16.9 0.8 add.427
  18.4 2.3 %fusion.27 = f32[4,256,128]{1,2,0:T(8,128)} fusion(bf16[256,4,128]{0,2,1:T(8,128)(2,1)} %bitcast.83, f32[4,256,256]{2,1,0:T(8,128)S(1)} %fusion.3, pred[256,256]{1,0:T(8,128)(4,1)S(1)} %get-tuple-element.10), kind=kOutput, calls=%fused_computation.68 | convolution fusion | flops 68943872 | bytes 1900544 | tf_op jit(solution)/shard_map/ghqk,gqhd->gkhd/dot_general | solution.py:43
  20.6 1.6 fusion.5
  22.3 1.0 fusion.33
  24.8 1.3 add.437
  26.1 2.1 %add.438 = f32[4,256,256]{2,1,0:T(8,128)S(1)} reshape(f32[4,2,128,2,128]{4,3,2,1,0:T(2,128)} %add.437) | data formatting | bytes 2097152 | tf_op jit(solution)/shard_map/add | solution.py:37
  28.2 2.1 %convolution_multiply_fusion.11 = f32[4,256,128]{1,2,0:T(8,128)} fusion(bf16[256,4,128]{0,2,1:T(8,128)(2,1)} %copy.171, f32[4,256,256]{2,1,0:T(8,128)S(1)} %fusion.5), kind=kOutput, calls=%fused_computation.40 | convolution fusion | flops 67502080 | bytes 1835008 | tf_op jit(solution)/shard_map/ghqk,gkhd->gqhd/dot_general | solution.py:54
  30.3 2.0 %copy.181 = f32[256,512]{1,0:T(8,128)} copy(f32[256,512]{0,1:T(8,128)} %bitcast.209) | data formatting | bytes 1048576 | tf_op jit(solution)/shard_map/squeeze;reshape | solution.py:118
  33.3 1.3 collective-permute-start.9
  34.8 1.9 %collective-permute-start.5 = (bf16[256,512]{0,1:T(8,128)(2,1)S(1)}, bf16[256,512]{0,1:T(8,128)(2,1)}, u32[]{:S(2)}, u32[]{:S(2)}) collective-permute-start(bf16[256,512]{0,1:T(8,128)(2,1)S(1)} %bitcast.194), channel_id=1, source_target_pairs={{2,0},{3,1},{4,2},{5,3},{6,4},{7,5},{10,8},{11,9},{12,10},{13,11},... | collective-permute-start | bytes 786440 | tf_op jit(solution)/shard_map/ppermute | solution.py:16
  41.8 0.8 copy.183
  42.8 0.8 copy.193
  43.8 11.8 %collective-permute-done.5 = bf16[256,512]{0,1:T(8,128)(2,1)} collective-permute-done((bf16[256,512]{0,1:T(8,128)(2,1)S(1)}, bf16[256,512]{0,1:T(8,128)(2,1)}, u32[]{:S(2)}, u32[]{:S(2)}) %collective-permute-start.5) | collective-permute-done | bytes 262176 | tf_op jit(solution)/shard_map/ppermute | solution.py:16
  55.6 2.1 %collective-permute-start.1 = (bf16[256,512]{0,1:T(8,128)(2,1)S(1)}, bf16[256,512]{0,1:T(8,128)(2,1)S(1)}, u32[]{:S(2)}, u32[]{:S(2)}) collective-permute-start(bf16[256,512]{0,1:T(8,128)(2,1)S(1)} %bitcast.195), channel_id=1, source_target_pairs={{1,0},{2,1},{3,2},{4,3},{5,4},{6,5},{7,6},{9,8},{10,9},{11,10},{12... | collective-permute-start | bytes 786440 | tf_op jit(solution)/shard_map/ppermute | solution.py:16
  57.7 1.0 reshape.841
  59.7 1.9 %reshape.840 = bf16[2,128,4,128]{1,0,3,2:T(2,128)(2,1)} reshape(bf16[256,512]{0,1:T(8,128)(2,1)} %collective-permute-done.4) | data formatting | bytes 524288 | tf_op jit(solution)/shard_map/reshape;reshape | solution.py:28
  61.7 2.1 %fusion.107 = (f32[2,4]{1,0:T(2,128)}, bf16[2,4,128,128]{2,3,1,0:T(8,128)(2,1)S(1)}) fusion(f32[2,4,128,128]{2,3,1,0:T(8,128)S(1)} %fusion.19, bf16[2,128,4,128]{1,3,2,0:T(8,128)(2,1)} %bitcast.221, bf16[2,128,4,128]{1,0,3,2:T(2,128)(2,1)} %reshape.840, pred[2,128,128]{1,2,0:T(8,128)(4,1)S(1)} %and_and_fusion.1), kind=kOutput, calls=%fused_computation.191 | convolution fusion | flops 35127288 | bytes 1343520 | tf_op jit(solution)/shard_map/gqhd,gkhd->ghqk/dot_general | solution.py:46
  64.1 1.0 fusion.17
  65.1 1.0 reshape.843
  67.1 1.9 %reshape.842 = bf16[2,128,4,128]{1,0,3,2:T(2,128)(2,1)} reshape(bf16[256,512]{0,1:T(8,128)(2,1)} %collective-permute-done.8) | data formatting | bytes 524288 | tf_op jit(solution)/shard_map/reshape;reshape | solution.py:28
  69.0 2.1 %fusion.108 = (f32[2,4]{1,0:T(2,128)}, bf16[2,4,128,128]{2,3,1,0:T(8,128)(2,1)S(1)}) fusion(f32[2,4,128,128]{2,3,1,0:T(8,128)S(1)} %fusion.16, bf16[2,128,4,128]{1,3,2,0:T(8,128)(2,1)} %bitcast.220, bf16[2,128,4,128]{1,0,3,2:T(2,128)(2,1)} %reshape.842, pred[2,128,128]{1,2,0:T(8,128)(4,1)S(1)} %and_and_fusion), kind=kOutput, calls=%fused_computation.192 | convolution fusion | flops 35127288 | bytes 1343520 | tf_op jit(solution)/shard_map/gqhd,gkhd->ghqk/dot_general | solution.py:46
  71.1 1.1 fusion.12
  72.2 1.1 fusion.36
  73.8 1.0 fusion.14
  75.4 1.1 fusion.37
  76.6 1.6 fusion.2
  78.2 1.1 convolution_multiply_fusion.10
  79.8 1.3 copy.219
  81.1 1.1 fusion.71
  82.3 2.0 %copy.191 = f32[2,128,4,128]{3,2,1,0:T(4,128)} copy(f32[2,128,4,128]{1,3,2,0:T(8,128)} %fusion.17) | data formatting | bytes 1048576 | tf_op jit(solution)/shard_map/mul | solution.py:54
  84.3 1.9 %copy.293 = f32[32,8,4,128]{3,1,2,0:T(8,128)} copy(f32[32,8,4,128]{3,2,1,0:T(4,128)} %bitcast.210) | data formatting | bytes 1048576
  86.2 1.0 copy.206
  87.2 1.3 copy.207
  88.5 1.1 fusion.73
  89.7 2.0 %copy.224 = f32[2,128,512]{2,0,1:T(2,128)} copy(f32[2,128,512]{1,2,0:T(8,128)} %bitcast.217) | data formatting | bytes 1048576 | tf_op jit(solution)/shard_map/reshape | solution.py:64
  91.7 2.1 %fusion.67 = f32[2,128,512]{2,0,1:T(2,128)S(1)} fusion(f32[2,128,512]{2,0,1:T(2,128)} %copy.224, s32[2]{0:T(128)S(1)} %get-tuple-element.8), kind=kOutput, calls=%fused_computation.125 | convolution fusion | flops 3145732 | bytes 1048584 | tf_op jit(solution)/shard_map/as,apc->spc/dot_general | solution.py:154
  93.8 0.9 copy.225
  94.7 2.0 %copy.201 = f32[2,128,4,128]{3,2,1,0:T(4,128)} copy(f32[2,128,4,128]{1,3,2,0:T(8,128)} %fusion.14) | data formatting | bytes 1048576 | tf_op jit(solution)/shard_map/mul | solution.py:54
  96.7 1.9 %copy.292 = f32[32,8,4,128]{3,1,2,0:T(8,128)} copy(f32[32,8,4,128]{3,2,1,0:T(4,128)} %bitcast.212) | data formatting | bytes 1048576
  98.6 2.0 %copy.213 = f32[2,128,4,128]{1,3,2,0:T(8,128)} copy(f32[2,128,4,128]{3,1,2,0:T(8,128)} %fusion.12) | data formatting | bytes 1048576 | tf_op jit(solution)/shard_map/mul | solution.py:58
  100.7 2.1 %copy.214 = f32[2,128,512]{2,0,1:T(2,128)} copy(f32[2,128,512]{1,2,0:T(8,128)} %bitcast.213) | data formatting | bytes 1048576 | tf_op jit(solution)/shard_map/reshape | solution.py:63
  102.7 2.2 %fusion.69 = f32[2,128,512]{2,0,1:T(2,128)S(1)} fusion(f32[2,128,512]{2,0,1:T(2,128)} %copy.214, s32[2]{0:T(128)S(1)} %get-tuple-element.8), kind=kOutput, calls=%fused_computation.127 | convolution fusion | flops 3145732 | bytes 1048584 | tf_op jit(solution)/shard_map/as,apc->spc/dot_general | solution.py:151
  104.9 0.9 copy.215
  105.8 3.1 %collective-permute-start.10 = (f32[256,512]{1,0:T(8,128)}, f32[256,512]{1,0:T(8,128)}, u32[]{:S(2)}, u32[]{:S(2)}) collective-permute-start(f32[256,512]{1,0:T(8,128)} %bitcast.181), channel_id=1, source_target_pairs={{0,4},{1,5},{2,6},{3,7},{8,12},{9,13},{10,14},{11,15},{16,20},{17,... | collective-permute-start | bytes 1572872 | tf_op jit(solution)/shard_map/ppermute | solution.py:16
  108.9 1.9 %collective-permute-start.6 = (f32[256,512]{1,0:T(8,128)}, f32[256,512]{1,0:T(8,128)}, u32[]{:S(2)}, u32[]{:S(2)}) collective-permute-start(f32[256,512]{1,0:T(8,128)} %bitcast.182), channel_id=1, source_target_pairs={{0,2},{1,3},{2,4},{3,5},{4,6},{5,7},{8,10},{9,11},{10,12},{11,13},... | collective-permute-start | bytes 1572872 | tf_op jit(solution)/shard_map/ppermute | solution.py:16
  110.9 2.2 %convolution_add_fusion = f32[4,256,128]{1,2,0:T(8,128)} fusion(f32[4,256,128]{1,2,0:T(8,128)S(1)} %copy-done.38, bf16[256,4,128]{0,2,1:T(8,128)(2,1)} %bitcast.9, f32[4,256,256]{2,1,0:T(8,128)S(1)} %copy-done.16, pred[256,256]{1,0:T(8,128)(4,1)S(1)} %get-tuple-element.9), kind=kOutput, calls=%fused_computation.36 | convolution fusion | flops 69074944 | bytes 2424832 | tf_op jit(solution)/shard_map/ghqk,gqhd->gkhd/dot_general | solution.py:43
  113.1 2.0 %copy.221 = f32[1,256,512]{2,1,0:T(8,128)} copy(f32[1,256,512]{1,2,0:T(8,128)} %bitcast.219) | data formatting | bytes 1048576 | tf_op jit(solution)/shard_map/add | solution.py:199
  115.1 2.1 %fusion.20 = f32[4,256,128]{1,2,0:T(8,128)} fusion(f32[4,256,128]{1,2,0:T(8,128)} %fusion.33, bf16[256,4,128]{0,2,1:T(8,128)(2,1)S(1)} %bitcast.216, f32[4,256,256]{2,1,0:T(8,128)S(1)} %fusion.2), kind=kOutput, calls=%fused_computation.38 | convolution fusion | flops 67633152 | bytes 2359296 | tf_op jit(solution)/shard_map/ghqk,gqhd->gkhd/dot_general | solution.py:58
  117.2 2.0 %copy.209 = f32[1,256,512]{2,1,0:T(8,128)} copy(f32[1,256,512]{1,2,0:T(8,128)} %bitcast.214) | data formatting | bytes 1048576 | tf_op jit(solution)/shard_map/add | solution.py:198
  120.3 1.0 copy.180
  123.3 23.5 %psum.14 = f32[4,7]{1,0:T(4,128)S(1)} all-reduce(f32[4,7]{1,0:T(4,128)S(1)} %convolution_add_fusion.2), channel_id=1, replica_groups=mesh['dp'=4,'ctx'=8] {'ctx'}, use_global_device_ids=true, to_apply=%region_4.6 | all-reduce | flops 28 | bytes 224 | tf_op jit(solution)/shard_map/psum | solution.py:203
  146.7 9.5 %psum.15 = f32[4,7]{1,0:T(4,128)} all-reduce(f32[4,7]{1,0:T(4,128)S(1)} %psum.14), channel_id=1, replica_groups=mesh['dp'=4,'ctx'=8] {'dp'}, use_global_device_ids=true, to_apply=%region_5.7 | all-reduce | flops 28 | bytes 224 | tf_op jit(solution)/shard_map/psum | solution.py:204
  156.2 1.9 %collective-permute-start.2 = (f32[256,512]{1,0:T(8,128)}, f32[256,512]{1,0:T(8,128)S(1)}, u32[]{:S(2)}, u32[]{:S(2)}) collective-permute-start(f32[256,512]{1,0:T(8,128)} %copy.180), channel_id=1, source_target_pairs={{0,1},{1,2},{2,3},{3,4},{4,5},{5,6},{6,7},{8,9},{9,10},{10,11},{11... | collective-permute-start | bytes 1572872 | tf_op jit(solution)/shard_map/ppermute | solution.py:16
  158.2 0.8 fusion.22
  159.5 0.8 fusion.23
  160.3 6.6 %collective-permute-done.2 = f32[256,512]{1,0:T(8,128)S(1)} collective-permute-done((f32[256,512]{1,0:T(8,128)}, f32[256,512]{1,0:T(8,128)S(1)}, u32[]{:S(2)}, u32[]{:S(2)}) %collective-permute-start.2) | collective-permute-done | bytes 524320 | tf_op jit(solution)/shard_map/ppermute | solution.py:16
  166.9 2.1 %fusion.30 = bf16[1,256,512]{2,1,0:T(8,128)(2,1)} fusion(f32[256,512]{1,0:T(8,128)} %collective-permute-done.10, f32[256,512]{1,0:T(8,128)} %collective-permute-done.6, f32[256,512]{1,0:T(8,128)S(1)} %copy-done.14, f32[256,512]{1,0:T(8,128)S(1)} %collective-permute-done.2), kind=kLoop, calls=%fused_computation.71 | loop fusion | flops 524288 | bytes 2359296 | tf_op jit(solution)/shard_map/convert_element_type | solution.py:206
  (142 shorter events, 19.2 us)
Async XLA Ops:
  0.6 12.8 %copy-start = (f32[4,7]{1,0:T(4,128)S(1)}, f32[4,7]{1,0:T(4,128)}, u32[]{:S(2)}) copy-start(f32[4,7]{1,0:T(4,128)} %param.17) | copy-start | bytes 340
  1.3 12.4 %copy-start.7 = (bf16[1,256,512]{2,1,0:T(8,128)(2,1)S(1)}, bf16[1,256,512]{2,1,0:T(8,128)(2,1)}, u32[]{:S(2)}) copy-start(bf16[1,256,512]{2,1,0:T(8,128)(2,1)} %param.11) | copy-start | bytes 786436
  1.3 31.4 %collective-permute-start.7 = (bf16[2,2]{1,0:T(2,128)(2,1)S(1)}, bf16[2,2]{1,0:T(2,128)(2,1)S(1)}, u32[]{:S(2)}, u32[]{:S(2)}) collective-permute-start(bf16[2,2]{1,0:T(2,128)(2,1)S(1)} %convert_bitcast_fusion), channel_id=1, source_target_pairs={{4,0},{5,1},{6,2},{7,3},{12,8},{13,9},{14,10},{15,11},{20,16},{21,... | collective-permute-start | bytes 32 | tf_op jit(solution)/shard_map/ppermute | solution.py:16
  2.8 32.0 %collective-permute-start.3 = (bf16[2,2]{1,0:T(2,128)(2,1)S(1)}, bf16[2,2]{1,0:T(2,128)(2,1)S(1)}, u32[]{:S(2)}, u32[]{:S(2)}) collective-permute-start(bf16[2,2]{1,0:T(2,128)(2,1)S(1)} %convert_bitcast_fusion), channel_id=1, source_target_pairs={{2,0},{3,1},{4,2},{5,3},{6,4},{7,5},{10,8},{11,9},{12,10},{13,11},... | collective-permute-start | bytes 32 | tf_op jit(solution)/shard_map/ppermute | solution.py:16
  6.9 60.2 %collective-permute-start.8 = (bf16[256,512]{0,1:T(8,128)(2,1)}, bf16[256,512]{0,1:T(8,128)(2,1)}, u32[]{:S(2)}, u32[]{:S(2)}) collective-permute-start(bf16[256,512]{0,1:T(8,128)(2,1)} %bitcast.8), channel_id=1, source_target_pairs={{4,0},{5,1},{6,2},{7,3},{12,8},{13,9},{14,10},{15,11},{20,16},{21,... | collective-permute-start | bytes 786440 | tf_op jit(solution)/shard_map/ppermute | solution.py:16
  8.2 51.5 %collective-permute-start.4 = (bf16[256,512]{0,1:T(8,128)(2,1)}, bf16[256,512]{0,1:T(8,128)(2,1)}, u32[]{:S(2)}, u32[]{:S(2)}) collective-permute-start(bf16[256,512]{0,1:T(8,128)(2,1)} %bitcast.8), channel_id=1, source_target_pairs={{2,0},{3,1},{4,2},{5,3},{6,4},{7,5},{10,8},{11,9},{12,10},{13,11},... | collective-permute-start | bytes 786440 | tf_op jit(solution)/shard_map/ppermute | solution.py:16
  10.1 66.4 %collective-permute-start = (bf16[256,512]{0,1:T(8,128)(2,1)}, bf16[256,512]{0,1:T(8,128)(2,1)}, u32[]{:S(2)}, u32[]{:S(2)}) collective-permute-start(bf16[256,512]{0,1:T(8,128)(2,1)} %bitcast.8), channel_id=1, source_target_pairs={{1,0},{2,1},{3,2},{4,3},{5,4},{6,5},{7,6},{9,8},{10,9},{11,10},{12... | collective-permute-start | bytes 786440 | tf_op jit(solution)/shard_map/ppermute | solution.py:16
  12.1 1.3 copy-start.34
  13.8 1.0 copy-start.21
  14.8 0.9 copy-start.5
  15.7 2.0 %copy-start.2 = (bf16[1,256,512]{1,2,0:T(8,128)(2,1)}, bf16[1,256,512]{1,2,0:T(8,128)(2,1)S(1)}, u32[]{:S(2)}) copy-start(bf16[1,256,512]{1,2,0:T(8,128)(2,1)S(1)} %copy.255) | copy-start | bytes 786436
  18.4 2.3 %copy-start.22 = (bf16[256,4,128]{2,1,0:T(4,128)(2,1)S(1)}, bf16[256,4,128]{2,1,0:T(4,128)(2,1)}, u32[]{:S(2)}) copy-start(bf16[256,4,128]{2,1,0:T(4,128)(2,1)} %reshape.770) | copy-start | bytes 786436
  20.6 1.6 copy-start.3
  23.9 0.6 copy-start.28
  32.3 0.9 copy-start.4
  32.3 4.6 %copy-start.6 = (bf16[1,256,512]{2,1,0:T(8,128)(2,1)S(1)}, bf16[1,256,512]{2,1,0:T(8,128)(2,1)}, u32[]{:S(2)}) copy-start(bf16[1,256,512]{2,1,0:T(8,128)(2,1)} %param.12) | copy-start | bytes 786436
  33.3 31.8 %collective-permute-start.9 = (bf16[256,512]{0,1:T(8,128)(2,1)S(1)}, bf16[256,512]{0,1:T(8,128)(2,1)}, u32[]{:S(2)}, u32[]{:S(2)}) collective-permute-start(bf16[256,512]{0,1:T(8,128)(2,1)S(1)} %bitcast.193), channel_id=1, source_target_pairs={{4,0},{5,1},{6,2},{7,3},{12,8},{13,9},{14,10},{15,11},{20,16},{21,... | collective-permute-start | bytes 786440 | tf_op jit(solution)/shard_map/ppermute | solution.py:16
  34.8 5.5 %copy-start.30 = (s32[2]{0:T(128)}, s32[2]{0:T(128)S(1)}, u32[]{:S(2)}) copy-start(s32[2]{0:T(128)S(1)} %get-tuple-element.15) | copy-start | bytes 28
  34.8 20.9 %collective-permute-start.5 = (bf16[256,512]{0,1:T(8,128)(2,1)S(1)}, bf16[256,512]{0,1:T(8,128)(2,1)}, u32[]{:S(2)}, u32[]{:S(2)}) collective-permute-start(bf16[256,512]{0,1:T(8,128)(2,1)S(1)} %bitcast.194), channel_id=1, source_target_pairs={{2,0},{3,1},{4,2},{5,3},{6,4},{7,5},{10,8},{11,9},{12,10},{13,11},... | collective-permute-start | bytes 786440 | tf_op jit(solution)/shard_map/ppermute | solution.py:16
  36.9 4.1 %copy-start.32 = (s32[2]{0:T(128)}, s32[2]{0:T(128)S(1)}, u32[]{:S(2)}) copy-start(s32[2]{0:T(128)S(1)} %get-tuple-element.11) | copy-start | bytes 28
  36.9 1.0 copy-start.8
  55.6 17.7 %collective-permute-start.1 = (bf16[256,512]{0,1:T(8,128)(2,1)S(1)}, bf16[256,512]{0,1:T(8,128)(2,1)S(1)}, u32[]{:S(2)}, u32[]{:S(2)}) collective-permute-start(bf16[256,512]{0,1:T(8,128)(2,1)S(1)} %bitcast.195), channel_id=1, source_target_pairs={{1,0},{2,1},{3,2},{4,3},{5,4},{6,5},{7,6},{9,8},{10,9},{11,10},{12... | collective-permute-start | bytes 786440 | tf_op jit(solution)/shard_map/ppermute | solution.py:16
  58.8 0.7 copy-start.27
  59.7 4.1 %copy-start.17 = (f32[2,4,128,128]{2,3,1,0:T(8,128)}, f32[2,4,128,128]{2,3,1,0:T(8,128)S(1)}, u32[]{:S(2)}) copy-start(f32[2,4,128,128]{2,3,1,0:T(8,128)S(1)} %fusion.19) | copy-start | bytes 1572868
  66.1 0.7 copy-start.26
  67.1 4.0 %copy-start.19 = (f32[2,4,128,128]{2,3,1,0:T(8,128)}, f32[2,4,128,128]{2,3,1,0:T(8,128)S(1)}, u32[]{:S(2)}) copy-start(f32[2,4,128,128]{2,3,1,0:T(8,128)S(1)} %fusion.16) | copy-start | bytes 1572868
  71.1 1.1 copy-start.18
  71.1 1.1 copy-start.24
  73.7 2.8 %copy-start.15 = (f32[4,256,256]{2,1,0:T(8,128)}, f32[4,256,256]{2,1,0:T(8,128)S(1)}, u32[]{:S(2)}) copy-start(f32[4,256,256]{2,1,0:T(8,128)S(1)} %fusion) | copy-start | bytes 3145732
  73.7 1.4 copy-start.20
  73.7 1.7 copy-start.25
  75.4 1.1 copy-start.23
  76.6 1.6 copy-start.1
  102.7 8.1 %copy-start.16 = (f32[4,256,256]{2,1,0:T(8,128)S(1)}, f32[4,256,256]{2,1,0:T(8,128)}, u32[]{:S(2)}) copy-start(f32[4,256,256]{2,1,0:T(8,128)} %copy-done.15) | copy-start | bytes 3145732
  104.9 5.9 %copy-start.38 = (f32[4,256,128]{1,2,0:T(8,128)S(1)}, f32[4,256,128]{1,2,0:T(8,128)}, u32[]{:S(2)}) copy-start(f32[4,256,128]{1,2,0:T(8,128)} %fusion.27) | copy-start | bytes 1572868
  105.8 54.5 %collective-permute-start.10 = (f32[256,512]{1,0:T(8,128)}, f32[256,512]{1,0:T(8,128)}, u32[]{:S(2)}, u32[]{:S(2)}) collective-permute-start(f32[256,512]{1,0:T(8,128)} %bitcast.181), channel_id=1, source_target_pairs={{0,4},{1,5},{2,6},{3,7},{8,12},{9,13},{10,14},{11,15},{16,20},{17,... | collective-permute-start | bytes 1572872 | tf_op jit(solution)/shard_map/ppermute | solution.py:16
  108.9 51.4 %collective-permute-start.6 = (f32[256,512]{1,0:T(8,128)}, f32[256,512]{1,0:T(8,128)}, u32[]{:S(2)}, u32[]{:S(2)}) collective-permute-start(f32[256,512]{1,0:T(8,128)} %bitcast.182), channel_id=1, source_target_pairs={{0,2},{1,3},{2,4},{3,5},{4,6},{5,7},{8,10},{9,11},{10,12},{11,13},... | collective-permute-start | bytes 1572872 | tf_op jit(solution)/shard_map/ppermute | solution.py:16
  119.2 0.7 copy-start.29
  119.2 1.0 copy-start.9
  119.2 2.1 %copy-start.35 = (s32[2,2]{1,0:T(2,128)S(1)}, s32[2,2]{1,0:T(2,128)}, u32[]{:S(2)}) copy-start(s32[2,2]{1,0:T(2,128)} %copy-done.34) | copy-start | bytes 52
  120.3 37.9 %copy-start.10 = (f32[2,128,512]{2,1,0:T(8,128)S(1)}, f32[2,128,512]{2,1,0:T(8,128)}, u32[]{:S(2)}) copy-start(f32[2,128,512]{2,1,0:T(8,128)} %copy.225) | copy-start | bytes 1572868
  120.3 37.9 %copy-start.12 = (f32[1,256,512]{2,1,0:T(8,128)S(1)}, f32[1,256,512]{2,1,0:T(8,128)}, u32[]{:S(2)}) copy-start(f32[1,256,512]{2,1,0:T(8,128)} %copy.221) | copy-start | bytes 1572868
  121.5 0.6 copy-start.33
  121.5 0.7 copy-start.36
  122.4 0.7 copy-start.31
  122.4 0.7 copy-start.37
  156.2 10.7 %collective-permute-start.2 = (f32[256,512]{1,0:T(8,128)}, f32[256,512]{1,0:T(8,128)S(1)}, u32[]{:S(2)}, u32[]{:S(2)}) collective-permute-start(f32[256,512]{1,0:T(8,128)} %copy.180), channel_id=1, source_target_pairs={{0,1},{1,2},{2,3},{3,4},{4,5},{5,6},{6,7},{8,9},{9,10},{10,11},{11... | collective-permute-start | bytes 1572872 | tf_op jit(solution)/shard_map/ppermute | solution.py:16
  158.2 1.0 copy-start.11
  158.2 1.3 copy-start.13
  159.5 7.5 %copy-start.14 = (f32[256,512]{1,0:T(8,128)S(1)}, f32[256,512]{1,0:T(8,128)}, u32[]{:S(2)}) copy-start(f32[256,512]{1,0:T(8,128)} %copy.181) | copy-start | bytes 1572868
